TPU v7x, 128 devices: a whole 4x4x4 slice. The times are simulated.
128 devices in a mesh: dp: 4 (over y), mp: 32 (over x, z, core).
Axes of the slice: x: 4, y: 4, z: 4, core: 2. Of those that a mesh axis runs over, the one named last changes fastest.
Arguments:
- residual_in: bfloat16 [512, 3584], P('dp', 'mp'), may hold values from -6 to 6
- pre_gain: float32 [3584], replicated, may hold values from 0.5 to 1.5
- post_gain: float32 [3584], replicated, may hold values from 0.5 to 1.5
- w_gate: bfloat16 [3584, 14336], P(None, 'mp'), may hold values from -0.09375 to 0.09375
- w_up: bfloat16 [3584, 14336], P(None, 'mp'), may hold values from -0.09375 to 0.09375
- w_down: bfloat16 [14336, 3584], P('mp'), may hold values from -0.046875 to 0.046875
- w_enc: bfloat16 [3584, 65536], P(None, ('dp', 'mp')), may hold values from -0.09375 to 0.09375
- b_enc: float32 [65536], P(('dp', 'mp')), may hold values from -2.5 to 2.5
- threshold: float32 [65536], P(('dp', 'mp')), may hold values from 0.1 to 1
- w_dec: bfloat16 [65536, 3584], P(('dp', 'mp')), may hold values from -0.0234375 to 0.0234375
- b_dec: float32 [3584], replicated, may hold values from -1.5 to 1.5
Outputs:
- loss_value: float32 [], replicated
- d_w_enc: bfloat16 [3584, 65536], P(None, ('dp', 'mp'))
- d_w_dec: bfloat16 [65536, 3584], P(('dp', 'mp'))
- d_b_enc: float32 [65536], P(('dp', 'mp'))
- d_threshold: float32 [65536], P(('dp', 'mp'))
- d_b_dec: float32 [3584], replicated
All inputs are finite; a program needn't handle non-finite values.
Results may differ from a plain program's by a relative error of at most 0.014.
The roundings to bfloat16 on the way count: a program that leaves them out, or rounds other values in their place, can miss the bound.
Values may be sent and summed in bfloat16 or wider, within the bound.
A program may use at most 128 MiB of HBM per device.

v0:
```python
import jax
import jax.numpy as jnp
from jax import lax
from jax.sharding import PartitionSpec as P

norm_eps = 1e-06
gate_band = 0.1
sparsity_coef = 0.05


def contract_first(left, right):
    return lax.dot_general(
        left, right, (((0,), (0,)), ((), ())), preferred_element_type=jnp.float32
    )


def local(
    residual_in, pre_gain, post_gain, w_gate, w_up, w_down, w_enc, b_enc, threshold, w_dec, b_dec
):
    full_rows = lax.all_gather(residual_in, "mp", axis=1, tiled=True)
    resid_wide = full_rows.astype(jnp.float32)
    normed = (
        resid_wide
        * lax.rsqrt(jnp.mean(resid_wide * resid_wide, axis=1, keepdims=True) + norm_eps)
        * pre_gain[None, :]
    ).astype(jnp.bfloat16)
    gate_out = jnp.dot(normed, w_gate, preferred_element_type=jnp.float32)
    up_out = jnp.dot(normed, w_up, preferred_element_type=jnp.float32)
    hidden = (jax.nn.gelu(gate_out, approximate=True) * up_out).astype(jnp.bfloat16)
    col_width = residual_in.shape[1]
    model_width = full_rows.shape[1]
    out_share = lax.psum_scatter(
        lax.dot_general(
            w_down, hidden, (((0,), (1,)), ((), ())), preferred_element_type=jnp.float32
        ),
        "mp",
        scatter_dimension=0,
        tiled=True,
    )
    total_sq = lax.psum(jnp.sum(out_share * out_share, axis=0), "mp")
    row_scale = lax.rsqrt(total_sq / model_width + norm_eps)
    my_cols = lax.axis_index("mp") * col_width
    gain_share = lax.dynamic_slice_in_dim(post_gain, my_cols, col_width, 0)
    mixed = residual_in.T.astype(jnp.float32) + out_share * row_scale[None, :] * gain_share[:, None]
    column_rows = lax.all_gather(mixed.astype(jnp.bfloat16), "mp", axis=0, tiled=True)
    h_cols = lax.all_gather(column_rows, "dp", axis=1, tiled=True)
    pre_act = contract_first(h_cols, w_enc) + b_enc[None, :]
    soft = jax.nn.sigmoid((pre_act - threshold[None, :]) / gate_band)
    feat_bf = (pre_act * soft).astype(jnp.bfloat16)
    gate_part = jnp.sum(soft)
    recon_part = lax.dot_general(
        w_dec, feat_bf, (((0,), (1,)), ((), ())), preferred_element_type=jnp.float32
    )
    recon_all, gate_total = lax.psum((recon_part, gate_part), ("dp", "mp"))
    error_t = recon_all + b_dec[:, None] - h_cols.astype(jnp.float32)
    grad_bdec = jnp.sum(error_t, axis=1)
    square_total = jnp.sum(error_t * error_t)
    err_bf = error_t.astype(jnp.bfloat16)
    loss_value = (0.5 * square_total + sparsity_coef * gate_total) / (
        h_cols.shape[0] * h_cols.shape[1]
    )
    grad_wdec = lax.dot_general(
        feat_bf, err_bf, (((0,), (1,)), ((), ())), preferred_element_type=jnp.float32
    ).astype(jnp.bfloat16)
    grad_feat = lax.dot_general(
        err_bf, w_dec, (((0,), (1,)), ((), ())), preferred_element_type=jnp.float32
    )
    slope = soft * (1.0 - soft) / gate_band
    side_term = (grad_feat * pre_act + sparsity_coef) * slope
    grad_pre = grad_feat * soft + side_term
    grad_thresh = -jnp.sum(side_term, axis=0)
    grad_benc = jnp.sum(grad_pre, axis=0)
    grad_wenc = jnp.dot(
        h_cols, grad_pre.astype(jnp.bfloat16), preferred_element_type=jnp.float32
    ).astype(jnp.bfloat16)
    return (loss_value, grad_wenc, grad_wdec, grad_benc, grad_thresh, grad_bdec)


def solution(mesh):
    placed = (
        P("dp", "mp"),
        P(),
        P(),
        P(None, "mp"),
        P(None, "mp"),
        P("mp", None),
        P(None, ("dp", "mp")),
        P(("dp", "mp")),
        P(("dp", "mp")),
        P(("dp", "mp"), None),
        P(),
    )
    return jax.shard_map(
        local,
        mesh=mesh,
        in_specs=placed,
        out_specs=(
            P(),
            P(None, ("dp", "mp")),
            P(("dp", "mp"), None),
            P(("dp", "mp")),
            P(("dp", "mp")),
            P(),
        ),
        check_vma=False,
    )
```

profile of v0, /device:TPU:1, one launch (start us, length us, event | category | flops | bytes accessed | tf_op | source)
XLA Modules:
  0.0 526.1 jit_solution(124205612583446622)
XLA Ops:
  7.2 0.0 copy-start
  7.2 0.0 reduce-scatter.4.cloned.1.call-start
  7.2 27.9 %all_gather.9 = bf16[128,3584]{0,1:T(8,128)(2,1)S(1)} all-gather(bf16[128,112]{0,1:T(8,128)(2,1)} %param.11), channel_id=1, replica_groups=mesh['dp'=4,'mp'=32] {'mp'}, dimensions={1}, use_global_device_ids=true | all-gather | bytes 946176 | tf_op jit(solution)/shard_map/all_gather | solution.py:20
  35.1 0.0 copy-start.1
  35.1 0.0 copy-start.3
  35.1 0.5 fusion.2
  35.6 0.4 copy-done.1
  36.0 3.1 fusion.20
  39.1 0.0 copy-done
  39.1 0.0 copy-done.3
  39.1 6.0 %convolution_bitcast_fusion.1 = f32[3584,128]{0,1:T(8,128)} fusion(bf16[448,3584]{1,0:T(8,128)(2,1)S(1)} %copy-done, f32[128,448]{0,1:T(8,128)S(1)} %fusion.20, bf16[3584,448]{0,1:T(8,128)(2,1)} %param.15, bf16[128,3584]{0,1:T(8,128)(2,1)} %copy-done.1, f32[3584]{0:T(1024)S(1)} %copy-done.3, f32[128]{0:T(128)S(1)} %add_rsqrt_fusion.1), kind=kOutput, calls=%fused_computation.5 | convolution fusion | flops 824033280 | bytes 9419264 | tf_op jit(solution)/shard_map/dot_general | solution.py:33
  45.1 0.0 copy-start.2
  45.1 2.7 copy.23
  47.8 0.0 reduce-scatter.4.cloned.1.call-update
  47.8 0.0 all-gather.2.cloned.1.call-start
  47.9 0.8 dynamic_slice.3
  48.6 75.3 %reduce-scatter.4.cloned.1.call-done = f32[112,128]{1,0:T(8,128)} async-done(((f32[3584,128]{1,0:T(8,128)}), f32[112,128]{1,0:T(8,128)}) %reduce-scatter.4.cloned.1.call-update) | async-done | bytes 57360 | tf_op jit(solution)/shard_map/reduce_scatter | solution.py:32
  123.9 0.9 copy.24
  124.8 0.1 multiply_reduce_fusion.1
  124.9 64.3 %psum.21 = f32[128]{0:T(128)S(1)} all-reduce(f32[128]{0:T(128)S(1)} %multiply_reduce_fusion.1), channel_id=1, replica_groups=mesh['dp'=4,'mp'=32] {'mp'}, use_global_device_ids=true, to_apply=%region_3.0 | all-reduce | flops 128 | bytes 1024 | tf_op jit(solution)/shard_map/psum | solution.py:40
  189.3 0.0 copy-done.2
  189.3 0.9 fusion.23
  190.2 25.7 %all_gather.10 = bf16[3584,128]{1,0:T(8,128)(2,1)} all-gather(bf16[112,128]{1,0:T(8,128)(2,1)S(1)} %fusion.23), channel_id=1, replica_groups=mesh['dp'=4,'mp'=32] {'mp'}, dimensions={0}, use_global_device_ids=true | all-gather | bytes 946176 | tf_op jit(solution)/shard_map/all_gather | solution.py:45
  215.9 2.2 copy.22
  218.1 0.0 all-gather.2.cloned.1.call-update
  218.1 0.0 copy-start.8
  218.1 0.2 all-reduce.2.cloned.1.call-start
  218.3 42.6 %all-gather.2.cloned.1.call-done = bf16[3584,512]{0,1:T(8,128)(2,1)} async-done(((bf16[3584,128]{0,1:T(8,128)(2,1)}), bf16[3584,512]{0,1:T(8,128)(2,1)}) %all-gather.2.cloned.1.call-update) | async-done | bytes 3670032 | tf_op jit(solution)/shard_map/all_gather | solution.py:46
  260.9 0.0 copy-done.7
  260.9 0.0 copy-start.5
  260.9 5.3 %convolution_add_fusion = f32[512,512]{1,0:T(8,128)S(1)} fusion(bf16[3584,512]{0,1:T(8,128)(2,1)} %all-gather.2.cloned.1.call-done, bf16[3584,512]{1,0:T(8,128)(2,1)} %param.17, f32[512]{0:T(512)S(1)} %copy-done.7), kind=kOutput, calls=%fused_computation.14 | convolution fusion | flops 1879310336 | bytes 8390656 | tf_op jit(solution)/shard_map/dot_general | solution.py:12
  266.3 0.0 copy-start.9
  266.3 1.0 copy-done.9
  267.2 0.0 copy-done.8
  267.2 0.0 copy-done.5
  267.2 5.1 convolution_bitcast_fusion
  272.4 0.0 copy-start.4
  272.4 0.0 all-reduce.2.cloned.1.call-update
  272.4 160.2 %all-reduce.2.cloned.1.call-done = f32[3584,512]{0,1:T(8,128)} async-done(((f32[3584,512]{0,1:T(8,128)}), f32[3584,512]{0,1:T(8,128)}) %all-reduce.2.cloned.1.call-update) | async-done | bytes 7340048 | tf_op jit(solution)/shard_map/psum | solution.py:54
  432.6 0.0 copy-done.4
  432.6 5.9 %fusion = (f32[3584]{0:T(1024)}, f32[]{:T(128)}, bf16[3584,512]{0,1:T(8,128)(2,1)S(1)}) fusion(bf16[3584,512]{0,1:T(8,128)(2,1)} %all-gather.2.cloned.1.call-done, f32[3584,512]{0,1:T(8,128)} %all-reduce.2.cloned.1.call-done, f32[3584]{0:T(1024)S(1)} %copy-done.4), kind=kLoop, calls=%fused_computation.8 | loop fusion | flops 12841471 | bytes 14708740 | tf_op jit(solution)/shard_map/reduce_sum | solution.py:56
  438.6 0.0 copy-done.6
  438.6 0.0 copy-done.10
  438.6 3.9 fusion.25
  442.4 4.0 convolution_convert_fusion
  446.4 64.1 %psum.23 = f32[]{:T(128)} all-reduce(f32[]{:T(128)} %get-tuple-element.13), channel_id=1, replica_groups=mesh['dp'=4,'mp'=32] {'dp','mp'}, use_global_device_ids=true, to_apply=%region_7.0 | all-reduce | flops 1 | bytes 8 | tf_op jit(solution)/shard_map/psum | solution.py:54
  510.5 0.6 neg.7
  512.4 6.1 %convolution_convert_fusion.1 = bf16[3584,512]{1,0:T(8,128)(2,1)} fusion(bf16[3584,512]{0,1:T(8,128)(2,1)} %all-gather.2.cloned.1.call-done, bf16[512,512]{1,0:T(8,128)(2,1)} %get-tuple-element.11), kind=kOutput, calls=%fused_computation.4 | convolution fusion | flops 1880883200 | bytes 7864320 | tf_op jit(solution)/shard_map/dot_general | solution.py:73
  (5 shorter events, 0.0 us)
Async XLA Ops:
  7.2 31.9 %copy-start = (bf16[448,3584]{1,0:T(8,128)(2,1)S(1)}, bf16[448,3584]{1,0:T(8,128)(2,1)}, u32[]{:S(2)}) copy-start(bf16[448,3584]{1,0:T(8,128)(2,1)} %param.16) | copy-start | bytes 9633796
  7.2 116.7 %reduce-scatter.4.cloned.1.call-start = ((), (), s32[]{:S(2)}) async-start(), calls=%async_computation.3 | async-start | bytes 1892352 | tf_op jit(solution)/shard_map/reduce_scatter | solution.py:32
  35.1 0.9 copy-start.1
  35.1 4.0 copy-start.3
  45.1 144.2 %copy-start.2 = (bf16[128,112]{0,1:T(8,128)(2,1)S(1)}, bf16[128,112]{0,1:T(8,128)(2,1)}, u32[]{:S(2)}) copy-start(bf16[128,112]{0,1:T(8,128)(2,1)} %param.11) | copy-start | bytes 86020
  47.8 213.1 %copy-start.7 = (f32[512]{0:T(512)S(1)}, f32[512]{0:T(512)}, u32[]{:S(2)}) copy-start(f32[512]{0:T(512)} %param.18) | copy-start | bytes 6148
  47.8 213.1 %all-gather.2.cloned.1.call-start = ((), (), s32[]{:S(2)}) async-start(), calls=%async_computation.1 | async-start | bytes 4587520 | tf_op jit(solution)/shard_map/all_gather | solution.py:46
  218.1 49.1 %copy-start.8 = (f32[512]{0:T(512)S(1)}, f32[512]{0:T(512)}, u32[]{:S(2)}) copy-start(f32[512]{0:T(512)} %param.19) | copy-start | bytes 6148
  218.1 214.5 %all-reduce.2.cloned.1.call-start = ((), (), s32[]{:S(2)}) async-start(), calls=%async_computation.2 | async-start | bytes 14680064 | tf_op jit(solution)/shard_map/psum | solution.py:54
  260.9 6.3 %copy-start.5 = (bf16[512,3584]{1,0:T(8,128)(2,1)S(1)}, bf16[512,3584]{1,0:T(8,128)(2,1)}, u32[]{:S(2)}) copy-start(bf16[512,3584]{1,0:T(8,128)(2,1)} %param.20) | copy-start | bytes 11010052
  266.3 1.0 copy-start.9
  272.4 160.2 %copy-start.4 = (f32[3584]{0:T(1024)S(1)}, f32[3584]{0:T(1024)}, u32[]{:S(2)}) copy-start(f32[3584]{0:T(1024)} %param.21) | copy-start | bytes 43012
  432.6 6.0 %copy-start.6 = (bf16[512,3584]{1,0:T(8,128)(2,1)S(1)}, bf16[512,3584]{1,0:T(8,128)(2,1)}, u32[]{:S(2)}) copy-start(bf16[512,3584]{1,0:T(8,128)(2,1)} %param.20) | copy-start | bytes 11010052
  432.6 6.0 %copy-start.10 = (f32[512,512]{1,0:T(8,128)S(1)}, f32[512,512]{1,0:T(8,128)}, u32[]{:S(2)}) copy-start(f32[512,512]{1,0:T(8,128)} %copy-done.9) | copy-start | bytes 3145732
Sparse Core Ops, SparseCore 0:
  47.9 75.9 reduce-scatter.3
  218.2 42.6 all-gather.1
  272.5 160.0 all-reduce.1
where the time goes:
time: 527 us; the launch traced here: 526 us
  waiting for transfers between devices  278 us (53%)
  blocking collectives  182 us (35%)
  matrix products  33.4 us (6%)
  between operations  16.3 us (3%)
  local copies, waits for them, and re-layouts  8.05 us (2%)
  other arithmetic  8.04 us (2%)
    psum x1, waiting for transfers between devices, local(): recon_all, gate_total = lax.psum((recon_part, gate_part), ('dp', 'mp'))  160 us
    reduce_scatter x1, waiting for transfers between devices, local(): lax.psum_scatter(lax.dot_general(w_down, hidden, (((0,), (1,)), ((), ()))...  75.3 us
    psum x1, blocking collectives, local(): total_sq = lax.psum(jnp.sum(out_share * out_share, axis=0), 'mp')  64.3 us
    psum x1, blocking collectives, local(): recon_all, gate_total = lax.psum((recon_part, gate_part), ('dp', 'mp'))  64.1 us
    all_gather x1, waiting for transfers between devices, local(): h_cols = lax.all_gather(column_rows, 'dp', axis=1, tiled=True)  42.6 us
    all_gather x1, blocking collectives, local(): full_rows = lax.all_gather(residual_in, 'mp', axis=1, tiled=True)  27.9 us
    all_gather x1, blocking collectives, local(): lax.all_gather(mixed.astype(jnp.bfloat16), 'mp', axis=0, tiled=True)  25.7 us
  transfers between devices with their start and end apart: 3, of which 3 were waited for; matrix products, arithmetic and copies ran while one was open for 0% of the time, Pallas kernels for 0%

commit v1 on v0

--- a/solution.py
+++ b/solution.py
@@ -51,7 +51,7 @@
     recon_part = lax.dot_general(
         w_dec, feat_bf, (((0,), (1,)), ((), ())), preferred_element_type=jnp.float32
     )
-    recon_all, gate_total = lax.psum((recon_part, gate_part), ("dp", "mp"))
+    recon_all, gate_total = lax.psum(lax.psum((recon_part, gate_part), "mp"), "dp")
     error_t = recon_all + b_dec[:, None] - h_cols.astype(jnp.float32)
     grad_bdec = jnp.sum(error_t, axis=1)
     square_total = jnp.sum(error_t * error_t)

time: 527 us -> 645 us (1.22)
  waiting for transfers between devices: 278 us -> 382 us
  blocking collectives: 182 us -> 189 us
    psum x1 -> x2, waiting for transfers between devices: 160 us -> 264 us  [the longest x1 146 us: local(): lax.psum(lax.psum((recon_part, gate_part), 'mp'), 'dp')]
    psum x1 -> x2, blocking collectives: 64.1 us -> 70.6 us  [the longest x1 63.5 us: local(): lax.psum((recon_part, gate_part), 'mp')]
  transfers between devices with their start and end apart: 3 -> 4, of which waited for: 3 -> 4; matrix products, arithmetic and copies ran while one was open for 0% -> 0% of each run, Pallas kernels for 0% -> 0%
where the time goes in v1:
time: 645 us; the launch traced here: 639 us
  waiting for transfers between devices  382 us (59%)
  blocking collectives  189 us (29%)
  matrix products  35.8 us (6%)
  between operations  16.3 us (3%)
  local copies, waits for them, and re-layouts  8.04 us (1%)
  other arithmetic  8.04 us (1%)
    psum x1, waiting for transfers between devices, local(): lax.psum(lax.psum((recon_part, gate_part), 'mp'), 'dp')  146 us
    psum x1, waiting for transfers between devices, local(): lax.psum((recon_part, gate_part), 'mp')  118 us
    reduce_scatter x1, waiting for transfers between devices, local(): lax.psum_scatter(lax.dot_general(w_down, hidden, (((0,), (1,)), ((), ()))...  75.3 us
    psum x1, blocking collectives, local(): total_sq = lax.psum(jnp.sum(out_share * out_share, axis=0), 'mp')  64.3 us
    psum x1, blocking collectives, local(): lax.psum((recon_part, gate_part), 'mp')  63.5 us
    all_gather x1, waiting for transfers between devices, local(): h_cols = lax.all_gather(column_rows, 'dp', axis=1, tiled=True)  42.7 us
    all_gather x1, blocking collectives, local(): full_rows = lax.all_gather(residual_in, 'mp', axis=1, tiled=True)  27.9 us
    all_gather x1, blocking collectives, local(): lax.all_gather(mixed.astype(jnp.bfloat16), 'mp', axis=0, tiled=True)  25.7 us
  transfers between devices with their start and end apart: 4, of which 4 were waited for; matrix products, arithmetic and copies ran while one was open for 0% of the time, Pallas kernels for 0%

profile of v1, /device:TPU:1, one launch (start us, length us, event | category | flops | bytes accessed | tf_op | source)
XLA Modules:
  0.0 639.1 jit_solution(1904153193180739053)
XLA Ops:
  7.2 0.0 copy-start
  7.2 0.0 reduce-scatter.4.cloned.1.call-start
  7.2 27.9 %all_gather.9 = bf16[128,3584]{0,1:T(8,128)(2,1)S(1)} all-gather(bf16[128,112]{0,1:T(8,128)(2,1)} %param.11), channel_id=1, replica_groups=mesh['dp'=4,'mp'=32] {'mp'}, dimensions={1}, use_global_device_ids=true | all-gather | bytes 946176 | tf_op jit(solution)/shard_map/all_gather | solution.py:20
  35.1 0.5 fusion.2
  35.6 0.4 copy-done.1
  36.0 3.1 fusion.20
  39.1 0.0 copy-done
  39.1 0.0 copy-done.4
  39.1 6.0 convolution_bitcast_fusion.1
  45.1 2.7 copy.23
  47.8 0.0 reduce-scatter.4.cloned.1.call-update
  47.8 0.0 all-gather.2.cloned.1.call-start
  47.9 0.8 dynamic_slice.3
  48.6 75.3 %reduce-scatter.4.cloned.1.call-done = f32[112,128]{1,0:T(8,128)} async-done(((f32[3584,128]{1,0:T(8,128)}), f32[112,128]{1,0:T(8,128)}) %reduce-scatter.4.cloned.1.call-update) | async-done | bytes 57360 | tf_op jit(solution)/shard_map/reduce_scatter | solution.py:32
  123.9 0.9 copy.24
  124.8 0.1 multiply_reduce_fusion.1
  124.9 64.3 %psum.35 = f32[128]{0:T(128)S(1)} all-reduce(f32[128]{0:T(128)S(1)} %multiply_reduce_fusion.1), channel_id=1, replica_groups=mesh['dp'=4,'mp'=32] {'mp'}, use_global_device_ids=true, to_apply=%region_3.0 | all-reduce | flops 128 | bytes 1024 | tf_op jit(solution)/shard_map/psum | solution.py:40
  189.3 0.0 copy-done.3
  189.3 0.9 fusion.23
  190.2 25.7 %all_gather.10 = bf16[3584,128]{1,0:T(8,128)(2,1)} all-gather(bf16[112,128]{1,0:T(8,128)(2,1)S(1)} %fusion.23), channel_id=1, replica_groups=mesh['dp'=4,'mp'=32] {'mp'}, dimensions={0}, use_global_device_ids=true | all-gather | bytes 946176 | tf_op jit(solution)/shard_map/all_gather | solution.py:45
  215.9 2.2 copy.22
  218.1 0.0 all-gather.2.cloned.1.call-update
  218.1 0.0 copy-start.9
  218.1 0.0 all-reduce.3.cloned.1.call-start
  218.2 42.7 %all-gather.2.cloned.1.call-done = bf16[3584,512]{0,1:T(8,128)(2,1)} async-done(((bf16[3584,128]{0,1:T(8,128)(2,1)}), bf16[3584,512]{0,1:T(8,128)(2,1)}) %all-gather.2.cloned.1.call-update) | async-done | bytes 3670032 | tf_op jit(solution)/shard_map/all_gather | solution.py:46
  260.9 0.0 copy-done.8
  260.9 5.3 convolution_add_fusion
  266.3 0.0 copy-start.10
  266.3 0.9 copy-done.10
  267.2 0.0 copy-done.9
  267.2 0.0 copy-done.6
  267.2 5.1 convolution_bitcast_fusion
  272.4 0.0 all-reduce.3.cloned.1.call-update
  272.4 0.2 all-reduce.5.cloned.1.call-start
  272.6 118.3 %all-reduce.3.cloned.1.call-done = f32[3584,512]{0,1:T(8,128)} async-done(((f32[3584,512]{0,1:T(8,128)}), f32[3584,512]{0,1:T(8,128)}) %all-reduce.3.cloned.1.call-update) | async-done | bytes 7340048 | tf_op jit(solution)/shard_map/psum | solution.py:54
  390.9 0.0 all-reduce.5.cloned.1.call-update
  390.9 145.7 %all-reduce.5.cloned.1.call-done = f32[3584,512]{0,1:T(8,128)} async-done(((f32[3584,512]{0,1:T(8,128)}), f32[3584,512]{0,1:T(8,128)}) %all-reduce.5.cloned.1.call-update) | async-done | bytes 7340048 | tf_op jit(solution)/shard_map/psum | solution.py:54
  536.7 0.0 copy-done.5
  536.7 5.9 fusion
  542.6 0.0 copy-done.7
  542.6 0.0 copy-done.11
  542.6 3.9 fusion.25
  546.5 0.0 copy-done.2
  546.5 63.5 %psum.38 = f32[]{:T(128)} all-reduce(f32[]{:T(128)} %get-tuple-element.13), channel_id=1, replica_groups=mesh['dp'=4,'mp'=32] {'mp'}, use_global_device_ids=true, to_apply=%region_8.0 | all-reduce | flops 1 | bytes 8 | tf_op jit(solution)/shard_map/psum | solution.py:54
  610.0 6.3 convolution_convert_fusion
  616.3 7.2 %psum.39 = f32[]{:T(128)} all-reduce(f32[]{:T(128)} %psum.38), channel_id=1, replica_groups=mesh['dp'=4,'mp'=32] {'dp'}, use_global_device_ids=true, to_apply=%region_9.0 | all-reduce | flops 1 | bytes 8 | tf_op jit(solution)/shard_map/psum | solution.py:54
  623.5 0.6 neg.7
  625.3 6.1 convolution_convert_fusion.1
  (11 shorter events, 0.0 us)
Async XLA Ops:
  7.2 31.9 %copy-start = (bf16[448,3584]{1,0:T(8,128)(2,1)S(1)}, bf16[448,3584]{1,0:T(8,128)(2,1)}, u32[]{:S(2)}) copy-start(bf16[448,3584]{1,0:T(8,128)(2,1)} %param.16) | copy-start | bytes 9633796
  7.2 116.7 %reduce-scatter.4.cloned.1.call-start = ((), (), s32[]{:S(2)}) async-start(), calls=%async_computation.4 | async-start | bytes 1892352 | tf_op jit(solution)/shard_map/reduce_scatter | solution.py:32
  35.1 0.9 copy-start.1
  35.1 4.0 copy-start.4
  45.1 144.2 %copy-start.3 = (bf16[128,112]{0,1:T(8,128)(2,1)S(1)}, bf16[128,112]{0,1:T(8,128)(2,1)}, u32[]{:S(2)}) copy-start(bf16[128,112]{0,1:T(8,128)(2,1)} %param.11) | copy-start | bytes 86020
  47.8 213.1 %copy-start.8 = (f32[512]{0:T(512)S(1)}, f32[512]{0:T(512)}, u32[]{:S(2)}) copy-start(f32[512]{0:T(512)} %param.18) | copy-start | bytes 6148
  47.8 213.1 %all-gather.2.cloned.1.call-start = ((), (), s32[]{:S(2)}) async-start(), calls=%async_computation.1 | async-start | bytes 4587520 | tf_op jit(solution)/shard_map/all_gather | solution.py:46
  218.1 49.1 %copy-start.9 = (f32[512]{0:T(512)S(1)}, f32[512]{0:T(512)}, u32[]{:S(2)}) copy-start(f32[512]{0:T(512)} %param.19) | copy-start | bytes 6148
  218.1 172.8 %all-reduce.3.cloned.1.call-start = ((), (), s32[]{:S(2)}) async-start(), calls=%async_computation.2 | async-start | bytes 14680064 | tf_op jit(solution)/shard_map/psum | solution.py:54
  260.9 6.3 copy-start.6
  266.3 1.0 copy-start.10
  272.4 264.3 %all-reduce.5.cloned.1.call-start = ((), (), s32[]{:S(2)}) async-start(), calls=%async_computation.3 | async-start | bytes 14680064 | tf_op jit(solution)/shard_map/psum | solution.py:54
  390.9 145.7 %copy-start.5 = (f32[3584]{0:T(1024)S(1)}, f32[3584]{0:T(1024)}, u32[]{:S(2)}) copy-start(f32[3584]{0:T(1024)} %param.21) | copy-start | bytes 43012
  536.7 6.0 copy-start.7
  536.7 6.0 copy-start.11
  542.6 3.9 copy-start.2
Sparse Core Ops, SparseCore 0:
  47.9 75.9 reduce-scatter.3
  218.2 42.6 all-gather.1
  272.5 118.3 all-reduce.2
  393.1 143.4 all-reduce.4
